TPU v7x, 256 devices: a whole 4x4x8 slice. The times are simulated.
256 devices in a mesh: row: 16 (over x_hi, y, core), col: 16 (over x_lo, z).
Axes of the slice: x: 4 (x_hi: 2, x_lo: 2; x = x_hi * 2 + x_lo), y: 4, z: 8, core: 2. Of those that a mesh axis runs over, the one named last changes fastest.
Arguments:
- test_block: bfloat16 [512, 32768], P('col', 'row'), may hold values from -6 to 6
- inverse_gram: bfloat16 [32768, 32768], P('row', 'col'), may hold values from -0.03125 to 0.03125
- train_grads: bfloat16 [8192, 32768], P('col', 'row'), may hold values from -0.03125 to 0.03125
Outputs:
- scores: float32 [512, 8192], P('row', 'col')
All inputs are finite; a program needn't handle non-finite values.
Results may differ from a plain program's by a relative error of at most 0.0029.
Values may be sent and summed in bfloat16 or wider, within the bound.
A program may use at most 64 MiB of HBM per device.

v0:
```python
import jax
import jax.numpy as jnp
from jax import lax
from jax.sharding import PartitionSpec as P


def from_root(value, axis, source):
    kept = jnp.where(lax.axis_index(axis) == source, value, 0).astype(value.dtype)
    return lax.psum(kept, axis)


def body(test_block, inverse_gram, train_grads):
    partial_rows = jnp.dot(
        lax.all_gather(test_block, "col", axis=0, tiled=True),
        inverse_gram,
        preferred_element_type=jnp.float32,
    )
    summed = lax.psum(partial_rows, "row")
    conditioned = summed.astype(jnp.bfloat16)
    row_index = lax.axis_index("row")
    factor = lax.axis_size("row") // lax.axis_size("col")
    owner = row_index // factor
    held = from_root(conditioned, "col", owner)
    return lax.psum_scatter(
        lax.dot_general(
            held, train_grads, (((1,), (1,)), ((), ())), preferred_element_type=jnp.float32
        ),
        "row",
        scatter_dimension=0,
        tiled=True,
    )


def solution(mesh):
    return jax.shard_map(
        body,
        mesh=mesh,
        in_specs=(P("col", "row"), P("row", "col"), P("col", "row")),
        out_specs=P("row", "col"),
        check_vma=False,
    )
```

profile of v0, /device:TPU:1, one launch (start us, length us, event | category | flops | bytes accessed | tf_op | source)
XLA Modules:
  0.0 397.3 jit_solution(10009326601036413509)
XLA Ops:
  6.5 0.0 copy-start
  6.5 0.0 all-gather.2.cloned.1.call-start
  6.5 0.7 all-gather.2.cloned.1.call-update
  7.3 0.0 all-reduce.3.cloned.1.call-start
  7.3 67.5 %all-gather.2.cloned.1.call-done = bf16[512,2048]{1,0:T(8,128)(2,1)} async-done(((bf16[32,2048]{1,0:T(8,128)(2,1)}), bf16[512,2048]{1,0:T(8,128)(2,1)}) %all-gather.2.cloned.1.call-update) | async-done | bytes 2097168 | tf_op jit(solution)/shard_map/all_gather | solution.py:14
  74.8 10.4 %fusion = f32[512,2048]{1,0:T(8,128)} fusion(bf16[512,2048]{1,0:T(8,128)(2,1)} %all-gather.2.cloned.1.call-done, bf16[2048,2048]{1,0:T(8,128)(2,1)} %param.4), kind=kOutput, calls=%fused_computation.1 | convolution fusion | flops 4294967296 | bytes 14680064 | tf_op jit(solution)/shard_map/dot_general | solution.py:13
  85.3 88.1 %all-reduce.4 = bf16[512,2048]{1,0:T(8,128)(2,1)} all-reduce(f32[512,2048]{1,0:T(8,128)} %fusion), channel_id=1, replica_groups=mesh['row'=16,'col'=16] {'row'}, use_global_device_ids=true, to_apply=%region_0.0 | all-reduce | flops 1048576 | bytes 6291456 | tf_op jit(solution)/shard_map/psum | solution.py:18
  173.4 1.5 convert_select_fusion
  174.9 0.0 all-reduce.3.cloned.1.call-update
  174.9 0.0 reduce-scatter.2.cloned.1.call-start
  175.0 132.1 %all-reduce.3.cloned.1.call-done = bf16[512,2048]{1,0:T(8,128)(2,1)} async-done(((bf16[512,2048]{1,0:T(8,128)(2,1)}), bf16[512,2048]{1,0:T(8,128)(2,1)}) %all-reduce.3.cloned.1.call-update) | async-done | bytes 2097168 | tf_op jit(solution)/shard_map/psum | solution.py:9
  307.1 0.0 copy-done
  307.1 3.9 fusion.1
  310.9 0.0 reduce-scatter.2.cloned.1.call-update
  310.9 79.8 %reduce-scatter.2.cloned.1.call-done = f32[32,512]{1,0:T(8,128)} async-done(((f32[512,512]{1,0:T(8,128)}), f32[32,512]{1,0:T(8,128)}) %reduce-scatter.2.cloned.1.call-update) | async-done | bytes 65552 | tf_op jit(solution)/shard_map/reduce_scatter | solution.py:24
Async XLA Ops:
  6.5 300.5 %copy-start = (bf16[512,2048]{1,0:T(8,128)(2,1)S(1)}, bf16[512,2048]{1,0:T(8,128)(2,1)}, u32[]{:S(2)}) copy-start(bf16[512,2048]{1,0:T(8,128)(2,1)} %param.5) | copy-start | bytes 6291460
  6.5 68.3 %all-gather.2.cloned.1.call-start = ((), (), s32[]{:S(2)}) async-start(), calls=%async_computation.1 | async-start | bytes 2228224 | tf_op jit(solution)/shard_map/all_gather | solution.py:14
  7.3 299.8 %all-reduce.3.cloned.1.call-start = ((), (), s32[]{:S(2)}) async-start(), calls=%async_computation.2 | async-start | bytes 4194304 | tf_op jit(solution)/shard_map/psum | solution.py:9
  174.9 215.9 %reduce-scatter.2.cloned.1.call-start = ((), (), s32[]{:S(2)}) async-start(), calls=%async_computation.3 | async-start | bytes 1114112 | tf_op jit(solution)/shard_map/reduce_scatter | solution.py:24
Sparse Core Ops, SparseCore 0:
  9.1 65.6 all-gather.1
  175.0 131.9 all-reduce.2
  311.1 79.5 reduce-scatter.1
where the time goes:
time: 398 us; the launch traced here: 397 us
  waiting for transfers between devices  280 us (70%)
  blocking collectives  88.1 us (22%)
  matrix products  14.3 us (4%)
  between operations  13.1 us (3%)
    psum x1, waiting for transfers between devices, from_root(): return lax.psum(kept, axis)  132 us
    psum x1, blocking collectives, body(): summed = lax.psum(partial_rows, 'row')  88.1 us
    reduce_scatter x1, waiting for transfers between devices, body(): lax.psum_scatter(lax.dot_general(held, train_grads, (((1,), (1,)), ((), (...  79.8 us
    all_gather x1, waiting for transfers between devices, body(): lax.all_gather(test_block, 'col', axis=0, tiled=True)  67.5 us
    dot_general x1, matrix products, body(): jnp.dot(lax.all_gather(test_block, 'col', axis=0, tiled=True), inverse_gr...  10.4 us
  transfers between devices with their start and end apart: 3, of which 3 were waited for; matrix products, arithmetic and copies ran while one was open for 0% of the time, Pallas kernels for 0%

commit v1 on v0

v1 whole, which is shorter than its diff:
```python
import jax
import jax.numpy as jnp
from jax import lax
from jax.experimental import pallas as pl
from jax.experimental.pallas import tpu as pltpu
from jax.sharding import PartitionSpec as P

MESH = pl.DeviceIdType.MESH
A, C = 0, 1
CUT_A, CUT_C = 896, 112


def kernel(
    t_hbm, g_hbm, d_hbm, out_ref,
    tb, gb, db, part, xr, bs, br, ms, cb, s, dx, ds_, dr,
    load_sem, ag_send, ag_recv, x_send, x_recv, b_send, b_recv,
    m_send, m_recv, e_send, e_recv, d_send, d_recv,
):
    row, col = lax.axis_index("row"), lax.axis_index("col")
    j, k = row // 2, row % 2
    xl, z = col // 8, col % 8
    other = 1 - k

    def zdev(dz):
        return (row, xl * 8 + (z + dz) % 8)

    xdev = (row, (1 - xl) * 8 + z)
    coredev = (j * 2 + other, col)

    def plane(jj):
        return (jj * 2 + k, col)

    move_to = (col, (1 - k) * 8 + j)
    move_from = (2 * z + 1 - xl, row)

    loads = {}

    def load(name, src, dst, sem):
        c = pltpu.make_async_copy(src, dst, load_sem.at[sem])
        c.start()
        loads[name] = c

    def jt(t):
        return (j + 1 + t) % 8

    def slot(ph, mx, dz):
        zz, xx = (z + dz) % 8, jnp.where(mx, 1 - xl, xl)
        if ph == A:
            return (zz % 2) * 8 + xx * 4 + zz // 2
        return zz * 2 + 1 - xx

    load("t0", t_hbm.at[pl.ds(0, 16)], tb.at[0, pl.ds(pl.multiple_of(slot(A, False, 0) * 16, 16), 16)], 0)
    load("t1", t_hbm.at[pl.ds(16, 16)], tb.at[1, pl.ds(pl.multiple_of(slot(A, False, 0) * 16, 16), 16)], 1)
    for t in range(8):
        load(("g", t), g_hbm.at[:, pl.ds(pl.multiple_of(jt(t) * 256, 256), 256)], gb.at[jt(t)], 2 + t)
    for t in range(8):
        load(("d", t), d_hbm.at[:, pl.ds(t * 256, 256)], db.at[t], 10 + t)

    barrier = pltpu.get_barrier_semaphore()
    for to in [zdev(1), zdev(-1), xdev, coredev, move_from] + [plane((j + i) % 8) for i in range(1, 8)]:
        pl.semaphore_signal(barrier, inc=1, device_id=to, device_id_type=MESH)
    pl.semaphore_wait(barrier, 12)

    sent = []

    def remote(src, dst, ssem, rsem, to):
        return pltpu.make_async_remote_copy(
            src_ref=src, dst_ref=dst, send_sem=ssem, recv_sem=rsem, device_id=to, device_id_type=MESH
        )

    def start(c):
        c.start()
        sent.append(c)

    def block(ph, h, mx, dz, piece):
        sl = slot(ph, mx, dz)
        if ph == A:
            r = pl.ds(pl.multiple_of(sl * 16, 16), 16)
            if piece == "w":
                return tb.at[h, r]
            if piece == "xf":
                return tb.at[h, r, pl.ds(0, CUT_A)]
            return tb.at[h, r, pl.ds(CUT_A, 2048 - CUT_A)]
        if piece == "w":
            return cb.at[h, sl]
        if piece == "xf":
            return cb.at[h, sl, pl.ds(0, CUT_C)]
        return cb.at[h, sl, pl.ds(CUT_C, 256 - CUT_C)]

    def message(ph, h, kind, dr_, d):
        i = 2 * ph + h
        if kind == "X":
            dz, n = d, 16 + d % 8
            piece = "w" if d == 0 else "zf"
            return ((ph, h, False, dz, piece), (ph, h, True, dz, piece), i, n, xdev)
        sign = 1 if dr_ == 0 else -1
        mx, piece, n = (False, "w", 0) if kind == "W" else (True, "xf", 8)
        src = (ph, h, mx, -sign * (d - 1), piece)
        dst = (ph, h, mx, -sign * d, piece)
        return (src, dst, i, n + dr_ * 4 + d - 1, zdev(sign))

    def send(ph, h, kind, dr_, d):
        src, _, i, n, to = message(ph, h, kind, dr_, d)
        ref = block(*src)
        source = ref
        if ph == A and src[2] is False and src[3] == 0:
            source = t_hbm.at[pl.ds(16 * h, 16)]
        start(remote(source, ref, ag_send.at[i, n], ag_recv.at[i, n], to))

    def arrived(ph, h, kind, dr_, d):
        _, dst, i, n, to = message(ph, h, kind, dr_, d)
        ref = block(*dst)
        remote(ref, ref, ag_send.at[i, n], ag_recv.at[i, n], to).wait_recv()

    def exists(h, kind, dr_, d):
        return d <= 3 or (d == 4 and (dr_ == h) == (kind == "W"))

    def ag_start(ph, h):
        send(ph, h, "X", 0, 0)
        send(ph, h, "W", 0, 1)
        send(ph, h, "W", 1, 1)

    def ag_step(ph, h, d):
        if d == 0:
            arrived(ph, h, "X", 0, 0)
            for dr_ in (0, 1):
                send(ph, h, "P", dr_, 1)
            return
        for kind in ("W", "P"):
            for dr_ in (0, 1):
                if not exists(h, kind, dr_, d):
                    continue
                arrived(ph, h, kind, dr_, d)
                if exists(h, kind, dr_, d + 1):
                    send(ph, h, kind, dr_, d + 1)
                if kind == "W":
                    send(ph, h, "X", 0, -d if dr_ == 0 else d)

    def ag_x(ph, h, d):
        for dz in ((0,) if d == 0 else (-d, d) if d < 4 else (4 if h == 1 else -4,)):
            if dz != 0:
                arrived(ph, h, "X", 0, dz)

    def mm(h, t):
        if h == 0:
            loads[("g", t)].wait()
        jj = jt(t)
        p = jnp.dot(tb[h], gb[jj], preferred_element_type=jnp.float32)
        part[h, jj, 0] = p[:, :128]
        part[h, jj, 1] = p[:, 128:]
        start(remote(part.at[h, jj, other], xr.at[h, jj], x_send.at[h, t], x_recv.at[h, t], coredev))

    def ex(h, t):
        jj = jt(t)
        remote(part.at[h, jj, other], xr.at[h, jj], x_send.at[h, t], x_recv.at[h, t], coredev).wait_recv()
        if t < 7:
            bs[h, jj] = (part[h, jj, k] + xr[h, jj]).astype(jnp.bfloat16)
            start(remote(bs.at[h, jj], br.at[h, j], b_send.at[h, t], b_recv.at[h, t], plane(jj)))

    def b_red(h):
        acc = part[h, j, k] + xr[h, j]
        for t in range(7):
            jj = (j + 7 - t) % 8
            remote(bs.at[h, 0], br.at[h, jj], b_send.at[h, t], b_recv.at[h, t], plane(jj)).wait_recv()
            acc = acc + br[h, jj].astype(jnp.float32)
        ms[h] = acc.astype(jnp.bfloat16)
        start(remote(ms.at[h], cb.at[h, 2 * j + k], m_send.at[h], m_recv.at[h], move_to))

    def c_start(h):
        own = cb.at[h, slot(C, False, 0)]
        remote(ms.at[h], own, m_send.at[h], m_recv.at[h], move_to).wait_recv()
        ag_start(C, h)

    def mm2(h, d):
        ag_x(C, h, d)
        for dz in (0,) if d == 0 else (-d, d) if d < 4 else (4,):
            zz = (z + dz) % 8
            lhs = jnp.concatenate([cb[h, 2 * zz], cb[h, 2 * zz + 1]], axis=1)
            v = lax.dot_general(lhs, db[zz], (((1,), (1,)), ((), ())), preferred_element_type=jnp.float32)
            if d == 0:
                s[h] = v
            else:
                s[h] += v

    def half(q):
        return pl.ds(pl.multiple_of(q * 128, 128), 128)

    def d_copy(h):
        return remote(s.at[h, half(other)], dx.at[h], e_send.at[h], e_recv.at[h], coredev)

    def d_start(h):
        start(d_copy(h))

    def d_send_(h):
        d_copy(h).wait_recv()
        ds_[h] = s[h, half(k)] + dx[h]
        for t in range(7):
            jj = jt(t)
            start(remote(ds_.at[h, pl.ds(pl.multiple_of(jj * 16, 16), 16)], dr.at[h, j], d_send.at[h, t], d_recv.at[h, t], plane(jj)))

    def d_red(h):
        acc = ds_[h, pl.ds(pl.multiple_of(j * 16, 16), 16)]
        for t in range(7):
            jj = (j + 7 - t) % 8
            remote(dr.at[h, jj], dr.at[h, jj], d_send.at[h, t], d_recv.at[h, t], plane(jj)).wait_recv()
            acc = acc + dr[h, jj]
        out_ref[pl.ds(16 * h, 16)] = acc

    ag_start(A, 0)
    ag_step(A, 0, 0)
    ag_start(A, 1)
    ag_step(A, 0, 1)
    ag_step(A, 1, 0)
    ag_step(A, 0, 2)
    ag_step(A, 1, 1)
    ag_step(A, 0, 3)
    ag_step(A, 1, 2)
    ag_step(A, 0, 4)
    for d in range(1, 5):
        ag_x(A, 0, d)
    loads["t0"].wait()
    for t in range(8):
        mm(0, t)
        if t >= 2:
            ex(0, t - 2)
        if t == 3:
            ag_step(A, 1, 3)
        if t == 7:
            ag_step(A, 1, 4)
    for t in (6, 7):
        ex(0, t)
    for d in range(1, 5):
        ag_x(A, 1, d)
    loads["t1"].wait()
    for t in range(8):
        mm(1, t)
        if t >= 2:
            ex(1, t - 2)
    for t in (6, 7):
        ex(1, t)
    for t in range(8):
        loads[("d", t)].wait()
    b_red(0)
    c_start(0)
    ag_step(C, 0, 0)
    ag_step(C, 0, 1)
    b_red(1)
    mm2(0, 0)
    ag_step(C, 0, 2)
    c_start(1)
    mm2(0, 1)
    ag_step(C, 0, 3)
    ag_step(C, 1, 0)
    mm2(0, 2)
    ag_step(C, 0, 4)
    ag_step(C, 1, 1)
    mm2(0, 3)
    mm2(1, 0)
    mm2(0, 4)
    d_start(0)
    ag_step(C, 1, 2)
    mm2(1, 1)
    d_send_(0)
    ag_step(C, 1, 3)
    mm2(1, 2)
    ag_step(C, 1, 4)
    mm2(1, 3)
    mm2(1, 4)
    d_start(1)
    d_red(0)
    d_send_(1)
    d_red(1)
    for c in sent:
        c.wait_send()


def body(test_block, inverse_gram, train_grads):
    bf, f32 = jnp.bfloat16, jnp.float32
    dma = pltpu.SemaphoreType.DMA
    return pl.pallas_call(
        kernel,
        out_shape=jax.ShapeDtypeStruct((32, 512), f32),
        in_specs=[pl.BlockSpec(memory_space=pl.ANY)] * 3,
        out_specs=pl.BlockSpec(memory_space=pltpu.VMEM),
        scratch_shapes=[
            pltpu.VMEM((2, 256, 2048), bf),
            pltpu.VMEM((8, 2048, 256), bf),
            pltpu.VMEM((8, 512, 256), bf),
            pltpu.VMEM((2, 8, 2, 256, 128), f32),
            pltpu.VMEM((2, 8, 256, 128), f32),
            pltpu.VMEM((2, 8, 256, 128), bf),
            pltpu.VMEM((2, 8, 256, 128), bf),
            pltpu.VMEM((2, 256, 128), bf),
            pltpu.VMEM((2, 16, 256, 128), bf),
            pltpu.VMEM((2, 256, 512), f32),
            pltpu.VMEM((2, 128, 512), f32),
            pltpu.VMEM((2, 128, 512), f32),
            pltpu.VMEM((2, 8, 16, 512), f32),
            dma((18,)),
            dma((4, 24)), dma((4, 24)),
            dma((2, 8)), dma((2, 8)),
            dma((2, 8)), dma((2, 8)),
            dma((2,)), dma((2,)),
            dma((2,)), dma((2,)),
            dma((2, 8)), dma((2, 8)),
        ],
        compiler_params=pltpu.CompilerParams(
            collective_id=0, has_side_effects=True, vmem_limit_bytes=52 * 2**20
        ),
        cost_estimate=pl.CostEstimate(flops=5_400_000_000, bytes_accessed=11_000_000, transcendentals=0),
        name="scores_kernel",
    )(test_block, inverse_gram, train_grads)


def solution(mesh):
    return jax.shard_map(
        body,
        mesh=mesh,
        in_specs=(P("col", "row"), P("row", "col"), P("col", "row")),
        out_specs=P("row", "col"),
        check_vma=False,
    )
```

time: 398 us -> 105 us (0.26)
  waiting for transfers between devices: 280 us -> 0 us
  Pallas kernels: 0 us -> 103 us
  blocking collectives: 88.1 us -> 0 us
  matrix products: 14.3 us -> 0 us
  between operations: 13.1 us -> 0.01 us
    psum x1 -> x0, waiting for transfers between devices: 132 us -> none  [from_root(): return lax.psum(kept, axis)]
    pallas_call x0 -> x1, Pallas kernels: none -> 103 us  [body(): pl.pallas_call(kernel, out_shape=jax.ShapeDtypeStruct((32, 512), f32), in...]
    psum x1 -> x0, blocking collectives: 88.1 us -> none  [body(): summed = lax.psum(partial_rows, 'row')]
    reduce_scatter x1 -> x0, waiting for transfers between devices: 79.8 us -> none  [body(): lax.psum_scatter(lax.dot_general(held, train_grads, (((1,), (1,)), ((), (...]
    all_gather x1 -> x0, waiting for transfers between devices: 67.5 us -> none  [body(): lax.all_gather(test_block, 'col', axis=0, tiled=True)]
    dot_general x2 -> x0, matrix products: 14.3 us -> none  [the longest x1 10.4 us: body(): jnp.dot(lax.all_gather(test_block, 'col', axis=0, tiled=True), inverse_gr...]
  transfers between devices with their start and end apart: 3 -> 0, of which waited for: 3 -> 0; matrix products, arithmetic and copies ran while one was open for 0% -> 0% of each run, Pallas kernels for 0% -> 0%
where the time goes in v1:
time: 105 us
  Pallas kernels  103 us (98%)
  local copies, waits for them, and re-layouts  1.54 us (1%)
    pallas_call x1, Pallas kernels, body(): pl.pallas_call(kernel, out_shape=jax.ShapeDtypeStruct((32, 512), f32), in...  103 us

profile of v1, /device:TPU:1, one launch (start us, length us, event | category | flops | bytes accessed | tf_op | source)
XLA Modules:
  0.0 105.0 jit_solution(10508281762878078172)
XLA Ops:
  0.0 0.0 copy-start
  0.0 0.9 copy-done
  0.9 103.5 %scores_kernel.1 = f32[32,512]{1,0:T(8,128)S(1)} custom-call(bf16[32,2048]{1,0:T(8,128)(2,1)S(1)} %copy-done, bf16[2048,2048]{1,0:T(8,128)(2,1)} %g_hbm.1, bf16[512,2048]{1,0:T(8,128)(2,1)} %d_hbm.1), custom_call_target="tpu_custom_call" | custom-call | flops 5400000000 | bytes 11000000 | tf_op jit(solution)/shard_map/scores_kernel/pallas_call | solution.py:280
  104.4 0.6 copy.5
Async XLA Ops:
  0.0 0.9 copy-start

commit v2 on v0

v2 whole, which is shorter than its diff:
```python
import jax
import jax.numpy as jnp
from jax import lax
from jax.experimental import pallas as pl
from jax.experimental.pallas import tpu as pltpu
from jax.sharding import PartitionSpec as P

MESH = pl.DeviceIdType.MESH
A, C = 0, 1
CUT_A, CUT_C = 896, 112
NT = (((1,), (1,)), ((), ()))


def kernel(
    t_hbm, g_hbm, d_hbm, out_ref,
    tb, gb, db, own, bs, br, ms, cb, s, dx, ds_, dr,
    load_sem, ag_send, ag_recv, g_send, g_recv, f_send, f_recv, b_send, b_recv,
    m_send, m_recv, e_send, e_recv, d_send, d_recv,
):
    row, col = lax.axis_index("row"), lax.axis_index("col")
    j, k = row // 2, row % 2
    xh, y = j // 4, j % 4
    xl, z = col // 8, col % 8
    other = 1 - k
    sigma = 2 * y + xh
    u_own = (sigma + 4 * k) % 8

    def chip(sg):
        return (sg % 2) * 4 + sg // 2

    def zdev(dz):
        return (row, xl * 8 + (z + dz) % 8)

    def xzdev(dz):
        return (row, (1 - xl) * 8 + (z + dz) % 8)

    xdev = xzdev(0)
    coredev = (j * 2 + other, col)

    def plane(jj):
        return (jj * 2 + k, col)

    def turn(h, u):
        return u if h == 0 else (8 - u) % 8

    def move_to(h):
        return (col, ((1 - k + z) % 2) * 8 + (z + turn(h, u_own)) % 8)

    z_src = 2 * y + k

    def move_from(h):
        u = turn(h, (z - z_src) % 8)
        ks = (1 + xl + k) % 2
        return (chip((u + 4 * ks) % 8) * 2 + ks, xh * 8 + z_src)

    loads = {}

    def load(name, src, dst, sem):
        c = pltpu.make_async_copy(src, dst, load_sem.at[sem])
        c.start()
        loads[name] = c

    def tslot(h, c, mx, dz):
        zz, xx = (z + dz) % 8, jnp.where(mx, 1 - xl, xl)
        return tb.at[h, c, zz % 2, xx, zz // 2]

    def cslot(h, mx, dz):
        zz, xx = (z + dz) % 8, jnp.where(mx, 1 - xl, xl)
        return 2 * turn(h, (zz - z_src) % 8) + (1 + xx + k) % 2

    def tile(n):
        return (u_own // 2 + 1 + n) % 4

    for h in (0, 1):
        load(("t", h), t_hbm.at[pl.ds(16 * h, 16)], tslot(h, k, False, 0), h)
    for n in range(4):
        c0 = pl.multiple_of(k * 1024 + tile(n) * 256, 256)
        load(("g", n), g_hbm.at[:, pl.ds(c0, 256)], gb.at[k, tile(n)], 2 + n)
    for q in range(8):
        for kk in range(2):
            load(("d", q, kk), d_hbm.at[:, pl.ds(kk * 1024 + q * 128, 128)], db.at[q, :, pl.ds(kk * 128, 128)], 6 + 2 * q + kk)

    barrier = pltpu.get_barrier_semaphore()
    greet = [zdev(1), zdev(-1), xzdev(1), xzdev(-1), xdev, coredev, move_from(0), move_from(1)]
    for to in greet + [plane((j + i) % 8) for i in range(1, 8)]:
        pl.semaphore_signal(barrier, inc=1, device_id=to, device_id_type=MESH)
    pl.semaphore_wait(barrier, 15)

    sent = []

    def remote(src, dst, ssem, rsem, to):
        return pltpu.make_async_remote_copy(
            src_ref=src, dst_ref=dst, send_sem=ssem, recv_sem=rsem, device_id=to, device_id_type=MESH
        )

    def start(c):
        c.start()
        sent.append(c)

    def block(ph, h, mx, dz, piece, origin=False):
        if ph == A:
            cut = pl.ds(0, CUT_A) if piece == "x" else pl.ds(CUT_A, 2048 - CUT_A)
            if origin and not mx and dz == 0:
                return t_hbm.at[pl.ds(16 * h, 16), cut]
            return tslot(h, k, mx, dz).at[:, cut]
        cut = pl.ds(0, CUT_C) if piece == "x" else pl.ds(CUT_C, 256 - CUT_C)
        return cb.at[h, cslot(h, mx, dz), cut]

    def message(ph, h, kind, way, d):
        i = 2 * ph + h
        if kind in "XY":
            piece, n = ("z", 24 + d % 8) if kind == "X" else ("x", 32)
            return (ph, h, False, d, piece), (ph, h, True, d, piece), i, n, xdev
        sign = 1 if way == 0 else -1
        if kind == "E":
            return (ph, h, False, -sign * 3, "z"), (ph, h, True, -sign * 4, "z"), i, 28, xzdev(sign)
        mx, piece = kind == "p", "z" if kind == "z" else "x"
        n = "zxp".index(kind) * 8 + way * 4 + d - 1
        if kind == "p" and d == 1:
            return (ph, h, False, 0, piece), (ph, h, True, -sign, piece), i, n, xzdev(sign)
        return (ph, h, mx, -sign * (d - 1), piece), (ph, h, mx, -sign * d, piece), i, n, zdev(sign)

    def send(ph, h, kind, way, d):
        src, _, i, n, to = message(ph, h, kind, way, d)
        start(remote(block(*src, origin=True), block(*src), ag_send.at[i, n], ag_recv.at[i, n], to))

    def arrived(ph, h, kind, way, d):
        _, dst, i, n, to = message(ph, h, kind, way, d)
        ref = block(*dst)
        remote(ref, ref, ag_send.at[i, n], ag_recv.at[i, n], to).wait_recv()

    def exists(h, kind, way, d):
        return d <= 3 or (d == 4 and (way == h) == (kind != "p"))

    def ag_start(ph, h):
        for kind in "pzx":
            for way in (0, 1):
                send(ph, h, kind, way, 1)
        send(ph, h, "Y", 0, 0)
        send(ph, h, "X", 0, 0)

    def ag(ph, h, kind, d):
        for way in (0, 1):
            if exists(h, kind, way, d):
                arrived(ph, h, kind, way, d)
                if exists(h, kind, way, d + 1):
                    send(ph, h, kind, way, d + 1)
                if kind == "z" and d == 3 and way == h:
                    send(ph, h, "E", way, 4)
                if kind == "z" and d < 4:
                    send(ph, h, "X", 0, -d if way == 0 else d)

    def step(ph, h, d):
        for kind in "zpx":
            ag(ph, h, kind, d)

    def around(d):
        return (0,) if d == 0 else (-d, d) if d < 4 else (4,)

    def ag_x(ph, h, d):
        for dz in around(d):
            arrived(ph, h, "X", 0, dz)
        if d == 0:
            arrived(ph, h, "Y", 0, 0)

    def f_copy(h, dz):
        zz = (z + dz) % 8
        ref = tb.at[h, k, zz % 2, :, zz // 2]
        return remote(ref, ref, f_send.at[h, dz % 8], f_recv.at[h, dz % 8], coredev)

    def forward(h, d):
        ag_x(A, h, d)
        if d == 0:
            loads[("t", h)].wait()
        for dz in around(d):
            start(f_copy(h, dz))

    def forwarded(h):
        for dz in range(8):
            zz = (z + dz) % 8
            ref = tb.at[h, other, zz % 2, :, zz // 2]
            remote(ref, ref, f_send.at[h, dz], f_recv.at[h, dz], coredev).wait_recv()

    def g_copy(n):
        c0 = pl.multiple_of(other * 1024 + n * 256, 256)
        return remote(g_hbm.at[:, pl.ds(c0, 256)], gb.at[k, n], g_send.at[n], g_recv.at[n], coredev)

    def g_start():
        for n in range(4):
            start(g_copy(n))

    def g_wait():
        for n in range(4):
            loads[("g", n)].wait()
            remote(gb.at[other, n], gb.at[other, n], g_send.at[n], g_recv.at[n], coredev).wait_recv()

    def mm(h, n):
        nn = tile(n)
        p = jnp.dot(tb[h, 0].reshape(256, 2048), gb[0, nn], preferred_element_type=jnp.float32)
        p = p + jnp.dot(tb[h, 1].reshape(256, 2048), gb[1, nn], preferred_element_type=jnp.float32)
        for e in (0, 1):
            u = 2 * nn + e
            pe = p[:, e * 128 : e * 128 + 128]

            def away():
                bs[h, u] = pe.astype(jnp.bfloat16)
                b_copy(h, u).start()

            if n < 3:
                away()
            else:
                pl.when(u != u_own)(away)

                @pl.when(u == u_own)
                def _():
                    own[h] = pe

    def b_copy(h, u):
        sg = (u - 4 * k) % 8
        n = (sg - sigma) % 8
        return remote(bs.at[h, u], br.at[h, n], b_send.at[h, n], b_recv.at[h, n], plane(chip(sg)))

    def b_red(h):
        acc = own[h]
        for n in range(1, 8):
            remote(bs.at[h, 0], br.at[h, n], b_send.at[h, n], b_recv.at[h, n], coredev).wait_recv()
            acc = acc + br[h, n].astype(jnp.float32)
        ms[h] = acc.astype(jnp.bfloat16)
        start(remote(ms.at[h], cb.at[h, 2 * u_own + k], m_send.at[h], m_recv.at[h], move_to(h)))

    def c_start(h):
        here = cb.at[h, cslot(h, False, 0)]
        remote(here, here, m_send.at[h], m_recv.at[h], move_to(h)).wait_recv()
        ag_start(C, h)

    def mm2(h, d):
        ag_x(C, h, d)
        for dz in around(d):
            u = turn(h, (z + dz - z_src) % 8)
            lhs = jnp.concatenate([cb[h, 2 * u], cb[h, 2 * u + 1]], axis=1)
            v = lax.dot_general(lhs, db[u], NT, preferred_element_type=jnp.float32)
            if d == 0:
                s[h] = v
            else:
                s[h] += v

    def half(q):
        return pl.ds(pl.multiple_of(q * 128, 128), 128)

    def e_copy(h):
        return remote(s.at[h, half(other)], dx.at[h], e_send.at[h], e_recv.at[h], coredev)

    def d_copy(h, n):
        jj = (j + n) % 8
        rows = pl.ds(pl.multiple_of(jj * 16, 16), 16)
        return remote(ds_.at[h, rows], dr.at[h, n], d_send.at[h, n], d_recv.at[h, n], plane(jj))

    def d_out(h):
        e_copy(h).wait_recv()
        ds_[h] = s[h, half(k)] + dx[h]
        for n in range(1, 8):
            start(d_copy(h, n))

    def d_red(h):
        acc = ds_[h, pl.ds(pl.multiple_of(j * 16, 16), 16)]
        for n in range(1, 8):
            d_copy(h, n).wait_recv()
            acc = acc + dr[h, n]
        out_ref[pl.ds(16 * h, 16)] = acc

    ag_start(A, 0)
    for c in sent[2:4]:
        c.wait_send()
    del sent[2:4]
    ag_start(A, 1)
    g_start()
    step(A, 0, 1)
    step(A, 1, 1)
    forward(0, 0)
    step(A, 0, 2)
    forward(1, 0)
    step(A, 1, 2)
    forward(0, 1)
    step(A, 0, 3)
    forward(1, 1)
    step(A, 1, 3)
    forward(0, 2)
    step(A, 0, 4)
    forward(0, 3)
    forward(0, 4)
    step(A, 1, 4)
    forward(1, 2)
    g_wait()
    forwarded(0)
    mm(0, 0)
    forward(1, 3)
    forward(1, 4)
    mm(0, 1)
    mm(0, 2)
    mm(0, 3)
    forwarded(1)
    for n in range(4):
        mm(1, n)
    for c in loads:
        if c[0] == "d":
            loads[c].wait()
    b_red(0)
    b_red(1)
    c_start(0)
    step(C, 0, 1)
    c_start(1)
    mm2(0, 0)
    step(C, 0, 2)
    step(C, 1, 1)
    mm2(0, 1)
    mm2(1, 0)
    step(C, 0, 3)
    step(C, 1, 2)
    mm2(0, 2)
    mm2(1, 1)
    step(C, 0, 4)
    mm2(0, 3)
    mm2(0, 4)
    start(e_copy(0))
    step(C, 1, 3)
    mm2(1, 2)
    d_out(0)
    step(C, 1, 4)
    mm2(1, 3)
    mm2(1, 4)
    start(e_copy(1))
    d_red(0)
    d_out(1)
    d_red(1)
    for c in sent:
        c.wait_send()
    for h in (0, 1):
        for n in range(1, 8):
            remote(bs.at[h, 0], br.at[h, n], b_send.at[h, n], b_recv.at[h, n], coredev).wait_send()


def body(test_block, inverse_gram, train_grads):
    bf, f32 = jnp.bfloat16, jnp.float32
    dma = pltpu.SemaphoreType.DMA
    return pl.pallas_call(
        kernel,
        out_shape=jax.ShapeDtypeStruct((32, 512), f32),
        in_specs=[pl.BlockSpec(memory_space=pl.ANY)] * 3,
        out_specs=pl.BlockSpec(memory_space=pltpu.VMEM),
        scratch_shapes=[
            pltpu.VMEM((2, 2, 2, 2, 4, 16, 2048), bf),
            pltpu.VMEM((2, 4, 2048, 256), bf),
            pltpu.VMEM((8, 512, 256), bf),
            pltpu.VMEM((2, 256, 128), f32),
            pltpu.VMEM((2, 8, 256, 128), bf),
            pltpu.VMEM((2, 8, 256, 128), bf),
            pltpu.VMEM((2, 256, 128), bf),
            pltpu.VMEM((2, 16, 256, 128), bf),
            pltpu.VMEM((2, 256, 512), f32),
            pltpu.VMEM((2, 128, 512), f32),
            pltpu.VMEM((2, 128, 512), f32),
            pltpu.VMEM((2, 8, 16, 512), f32),
            dma((22,)),
            dma((4, 33)), dma((4, 33)),
            dma((4,)), dma((4,)),
            dma((2, 8)), dma((2, 8)),
            dma((2, 8)), dma((2, 8)),
            dma((2,)), dma((2,)),
            dma((2,)), dma((2,)),
            dma((2, 8)), dma((2, 8)),
        ],
        compiler_params=pltpu.CompilerParams(
            collective_id=0, has_side_effects=True, vmem_limit_bytes=52 * 2**20
        ),
        cost_estimate=pl.CostEstimate(flops=5_400_000_000, bytes_accessed=11_000_000, transcendentals=0),
        name="scores_kernel",
    )(test_block, inverse_gram, train_grads)


def solution(mesh):
    return jax.shard_map(
        body,
        mesh=mesh,
        in_specs=(P("col", "row"), P("row", "col"), P("col", "row")),
        out_specs=P("row", "col"),
        check_vma=False,
    )
```

time: 398 us -> 83.6 us (0.21)
  waiting for transfers between devices: 280 us -> 0 us
  blocking collectives: 88.1 us -> 0 us
  Pallas kernels: 0 us -> 82 us
  matrix products: 14.3 us -> 0 us
  between operations: 13.1 us -> 0.01 us
    psum x1 -> x0, waiting for transfers between devices: 132 us -> none  [from_root(): return lax.psum(kept, axis)]
    psum x1 -> x0, blocking collectives: 88.1 us -> none  [body(): summed = lax.psum(partial_rows, 'row')]
    pallas_call x0 -> x1, Pallas kernels: none -> 82 us  [body(): pl.pallas_call(kernel, out_shape=jax.ShapeDtypeStruct((32, 512), f32), in...]
    reduce_scatter x1 -> x0, waiting for transfers between devices: 79.8 us -> none  [body(): lax.psum_scatter(lax.dot_general(held, train_grads, (((1,), (1,)), ((), (...]
    all_gather x1 -> x0, waiting for transfers between devices: 67.5 us -> none  [body(): lax.all_gather(test_block, 'col', axis=0, tiled=True)]
    dot_general x2 -> x0, matrix products: 14.3 us -> none  [the longest x1 10.4 us: body(): jnp.dot(lax.all_gather(test_block, 'col', axis=0, tiled=True), inverse_gr...]
  transfers between devices with their start and end apart: 3 -> 0, of which waited for: 3 -> 0; matrix products, arithmetic and copies ran while one was open for 0% -> 0% of each run, Pallas kernels for 0% -> 0%
where the time goes in v2:
time: 83.6 us
  Pallas kernels  82 us (98%)
  local copies, waits for them, and re-layouts  1.54 us (2%)
    pallas_call x1, Pallas kernels, body(): pl.pallas_call(kernel, out_shape=jax.ShapeDtypeStruct((32, 512), f32), in...  82 us

profile of v2, /device:TPU:1, one launch (start us, length us, event | category | flops | bytes accessed | tf_op | source)
XLA Modules:
  0.0 83.6 jit_solution(17314529667940258433)
XLA Ops:
  0.0 0.0 copy-start
  0.0 0.9 %copy-done = bf16[32,2048]{1,0:T(8,128)(2,1)S(1)} copy-done((bf16[32,2048]{1,0:T(8,128)(2,1)S(1)}, bf16[32,2048]{1,0:T(8,128)(2,1)}, u32[]{:S(2)}) %copy-start) | copy-done | bytes 131096
  0.9 82.0 %scores_kernel.1 = f32[32,512]{1,0:T(8,128)S(1)} custom-call(bf16[32,2048]{1,0:T(8,128)(2,1)S(1)} %copy-done, bf16[2048,2048]{1,0:T(8,128)(2,1)} %g_hbm.1, bf16[512,2048]{1,0:T(8,128)(2,1)} %d_hbm.1), custom_call_target="tpu_custom_call" | custom-call | flops 5400000000 | bytes 11000000 | tf_op jit(solution)/shard_map/scores_kernel/pallas_call | solution.py:345
  82.9 0.6 copy.5
Async XLA Ops:
  0.0 0.9 %copy-start = (bf16[32,2048]{1,0:T(8,128)(2,1)S(1)}, bf16[32,2048]{1,0:T(8,128)(2,1)}, u32[]{:S(2)}) copy-start(bf16[32,2048]{1,0:T(8,128)(2,1)} %t_hbm.1) | copy-start | bytes 393220

commit v3 on v2

--- a/solution.py
+++ b/solution.py
@@ -7,13 +7,13 @@
 
 MESH = pl.DeviceIdType.MESH
 A, C = 0, 1
-CUT_A, CUT_C = 896, 112
+CUT_A, CUT_C = 1024, 128
 NT = (((1,), (1,)), ((), ()))
 
 
 def kernel(
     t_hbm, g_hbm, d_hbm, out_ref,
-    tb, gb, db, own, bs, br, ms, cb, s, dx, ds_, dr,
+    tb, gb, db, acc_, own, bs, br, ms, cb, s, dx, ds_, dr,
     load_sem, ag_send, ag_recv, g_send, g_recv, f_send, f_recv, b_send, b_recv,
     m_send, m_recv, e_send, e_recv, d_send, d_recv,
 ):
@@ -48,11 +48,6 @@
 
     z_src = 2 * y + k
 
-    def move_from(h):
-        u = turn(h, (z - z_src) % 8)
-        ks = (1 + xl + k) % 2
-        return (chip((u + 4 * ks) % 8) * 2 + ks, xh * 8 + z_src)
-
     loads = {}
 
     def load(name, src, dst, sem):
@@ -81,10 +76,10 @@
             load(("d", q, kk), d_hbm.at[:, pl.ds(kk * 1024 + q * 128, 128)], db.at[q, :, pl.ds(kk * 128, 128)], 6 + 2 * q + kk)
 
     barrier = pltpu.get_barrier_semaphore()
-    greet = [zdev(1), zdev(-1), xzdev(1), xzdev(-1), xdev, coredev, move_from(0), move_from(1)]
+    greet = [zdev(1), zdev(-1), xzdev(1), xzdev(-1), xdev, coredev]
     for to in greet + [plane((j + i) % 8) for i in range(1, 8)]:
         pl.semaphore_signal(barrier, inc=1, device_id=to, device_id_type=MESH)
-    pl.semaphore_wait(barrier, 15)
+    pl.semaphore_wait(barrier, 13)
 
     sent = []
 
@@ -191,13 +186,15 @@
 
     def g_wait():
         for n in range(4):
-            loads[("g", n)].wait()
             remote(gb.at[other, n], gb.at[other, n], g_send.at[n], g_recv.at[n], coredev).wait_recv()
+
+    def mma(h, n):
+        acc_[n] = jnp.dot(tb[h, k].reshape(256, 2048), gb[k, tile(n)], preferred_element_type=jnp.float32)
 
     def mm(h, n):
         nn = tile(n)
-        p = jnp.dot(tb[h, 0].reshape(256, 2048), gb[0, nn], preferred_element_type=jnp.float32)
-        p = p + jnp.dot(tb[h, 1].reshape(256, 2048), gb[1, nn], preferred_element_type=jnp.float32)
+        p = jnp.dot(tb[h, other].reshape(256, 2048), gb[other, nn], preferred_element_type=jnp.float32)
+        p = p + acc_[n]
         for e in (0, 1):
             u = 2 * nn + e
             pe = p[:, e * 128 : e * 128 + 128]
@@ -288,16 +285,19 @@
     step(A, 0, 4)
     forward(0, 3)
     forward(0, 4)
+    for n in range(4):
+        loads[("g", n)].wait()
+        mma(0, n)
     step(A, 1, 4)
     forward(1, 2)
     g_wait()
     forwarded(0)
-    mm(0, 0)
+    for n in range(4):
+        mm(0, n)
     forward(1, 3)
     forward(1, 4)
-    mm(0, 1)
-    mm(0, 2)
-    mm(0, 3)
+    for n in range(4):
+        mma(1, n)
     forwarded(1)
     for n in range(4):
         mm(1, n)
@@ -309,8 +309,8 @@
     c_start(0)
     step(C, 0, 1)
     c_start(1)
+    step(C, 0, 2)
     mm2(0, 0)
-    step(C, 0, 2)
     step(C, 1, 1)
     mm2(0, 1)
     mm2(1, 0)
@@ -329,8 +329,8 @@
     mm2(1, 3)
     mm2(1, 4)
     start(e_copy(1))
+    d_out(1)
     d_red(0)
-    d_out(1)
     d_red(1)
     for c in sent:
         c.wait_send()
@@ -351,6 +351,7 @@
             pltpu.VMEM((2, 2, 2, 2, 4, 16, 2048), bf),
             pltpu.VMEM((2, 4, 2048, 256), bf),
             pltpu.VMEM((8, 512, 256), bf),
+            pltpu.VMEM((4, 256, 256), f32),
             pltpu.VMEM((2, 256, 128), f32),
             pltpu.VMEM((2, 8, 256, 128), bf),
             pltpu.VMEM((2, 8, 256, 128), bf),

time: 83.6 us -> 81.3 us (0.972)
  Pallas kernels: 82 us -> 79.7 us
    pallas_call x1, Pallas kernels: 82 us -> 79.7 us  [body(): pl.pallas_call(kernel, out_shape=jax.ShapeDtypeStruct((32, 512), f32), in...]
where the time goes in v3:
time: 81.3 us; the launch traced here: 81.2 us
  Pallas kernels  79.7 us (98%)
  local copies, waits for them, and re-layouts  1.54 us (2%)
    pallas_call x1, Pallas kernels, body(): pl.pallas_call(kernel, out_shape=jax.ShapeDtypeStruct((32, 512), f32), in...  79.7 us

profile of v3, /device:TPU:1, one launch (start us, length us, event | category | flops | bytes accessed | tf_op | source)
XLA Modules:
  0.0 81.2 jit_solution(5867664937801237275)
XLA Ops:
  0.0 0.0 copy-start
  0.0 0.9 %copy-done = bf16[32,2048]{1,0:T(8,128)(2,1)S(1)} copy-done((bf16[32,2048]{1,0:T(8,128)(2,1)S(1)}, bf16[32,2048]{1,0:T(8,128)(2,1)}, u32[]{:S(2)}) %copy-start) | copy-done | bytes 131096
  0.9 79.7 %scores_kernel.1 = f32[32,512]{1,0:T(8,128)S(1)} custom-call(bf16[32,2048]{1,0:T(8,128)(2,1)S(1)} %copy-done, bf16[2048,2048]{1,0:T(8,128)(2,1)} %g_hbm.1, bf16[512,2048]{1,0:T(8,128)(2,1)} %d_hbm.1), custom_call_target="tpu_custom_call" | custom-call | flops 5400000000 | bytes 11000000 | tf_op jit(solution)/shard_map/scores_kernel/pallas_call | solution.py:345
  80.6 0.6 copy.5
Async XLA Ops:
  0.0 0.9 %copy-start = (bf16[32,2048]{1,0:T(8,128)(2,1)S(1)}, bf16[32,2048]{1,0:T(8,128)(2,1)}, u32[]{:S(2)}) copy-start(bf16[32,2048]{1,0:T(8,128)(2,1)} %t_hbm.1) | copy-start | bytes 393220

commit v4 on v3

--- a/solution.py
+++ b/solution.py
@@ -48,6 +48,11 @@
 
     z_src = 2 * y + k
 
+    barrier = pltpu.get_barrier_semaphore()
+    greet = [zdev(1), zdev(-1), xzdev(1), xzdev(-1), xdev, coredev]
+    for to in greet + [plane((j + i) % 8) for i in range(1, 8)]:
+        pl.semaphore_signal(barrier, inc=1, device_id=to, device_id_type=MESH)
+
     loads = {}
 
     def load(name, src, dst, sem):
@@ -75,13 +80,15 @@
         for kk in range(2):
             load(("d", q, kk), d_hbm.at[:, pl.ds(kk * 1024 + q * 128, 128)], db.at[q, :, pl.ds(kk * 128, 128)], 6 + 2 * q + kk)
 
-    barrier = pltpu.get_barrier_semaphore()
-    greet = [zdev(1), zdev(-1), xzdev(1), xzdev(-1), xdev, coredev]
-    for to in greet + [plane((j + i) % 8) for i in range(1, 8)]:
-        pl.semaphore_signal(barrier, inc=1, device_id=to, device_id_type=MESH)
     pl.semaphore_wait(barrier, 13)
 
     sent = []
+
+    def drain(keep):
+        n = max(len(sent) - keep, 0)
+        for c in sent[:n]:
+            c.wait_send()
+        del sent[:n]
 
     def remote(src, dst, ssem, rsem, to):
         return pltpu.make_async_remote_copy(
@@ -217,6 +224,10 @@
         n = (sg - sigma) % 8
         return remote(bs.at[h, u], br.at[h, n], b_send.at[h, n], b_recv.at[h, n], plane(chip(sg)))
 
+    def b_left(h):
+        for n in range(1, 8):
+            remote(bs.at[h, 0], br.at[h, n], b_send.at[h, n], b_recv.at[h, n], coredev).wait_send()
+
     def b_red(h):
         acc = own[h]
         for n in range(1, 8):
@@ -266,13 +277,10 @@
         out_ref[pl.ds(16 * h, 16)] = acc
 
     ag_start(A, 0)
-    for c in sent[2:4]:
-        c.wait_send()
-    del sent[2:4]
     ag_start(A, 1)
-    g_start()
     step(A, 0, 1)
     step(A, 1, 1)
+    g_start()
     forward(0, 0)
     step(A, 0, 2)
     forward(1, 0)
@@ -304,6 +312,7 @@
     for c in loads:
         if c[0] == "d":
             loads[c].wait()
+    drain(0)
     b_red(0)
     b_red(1)
     c_start(0)
@@ -325,6 +334,9 @@
     step(C, 1, 3)
     mm2(1, 2)
     d_out(0)
+    b_left(0)
+    b_left(1)
+    drain(40)
     step(C, 1, 4)
     mm2(1, 3)
     mm2(1, 4)
@@ -334,9 +346,6 @@
     d_red(1)
     for c in sent:
         c.wait_send()
-    for h in (0, 1):
-        for n in range(1, 8):
-            remote(bs.at[h, 0], br.at[h, n], b_send.at[h, n], b_recv.at[h, n], coredev).wait_send()
 
 
 def body(test_block, inverse_gram, train_grads):

time: 81.3 us -> 80.6 us (level)
  no operation moved by 1% of the time
where the time goes in v4:
time: 80.6 us; the launch traced here: 80.5 us
  Pallas kernels  78.9 us (98%)
  local copies, waits for them, and re-layouts  1.54 us (2%)
    pallas_call x1, Pallas kernels, body(): pl.pallas_call(kernel, out_shape=jax.ShapeDtypeStruct((32, 512), f32), in...  78.9 us

profile of v4, /device:TPU:1, one launch (start us, length us, event | category | flops | bytes accessed | tf_op | source)
XLA Modules:
  0.0 80.5 jit_solution(9062870762454269645)
XLA Ops:
  0.0 0.0 copy-start
  0.0 0.9 %copy-done = bf16[32,2048]{1,0:T(8,128)(2,1)S(1)} copy-done((bf16[32,2048]{1,0:T(8,128)(2,1)S(1)}, bf16[32,2048]{1,0:T(8,128)(2,1)}, u32[]{:S(2)}) %copy-start) | copy-done | bytes 131096
  0.9 78.9 %scores_kernel.1 = f32[32,512]{1,0:T(8,128)S(1)} custom-call(bf16[32,2048]{1,0:T(8,128)(2,1)S(1)} %copy-done, bf16[2048,2048]{1,0:T(8,128)(2,1)} %g_hbm.1, bf16[512,2048]{1,0:T(8,128)(2,1)} %d_hbm.1), custom_call_target="tpu_custom_call" | custom-call | flops 5400000000 | bytes 11000000 | tf_op jit(solution)/shard_map/scores_kernel/pallas_call | solution.py:354
  79.8 0.6 copy.5
Async XLA Ops:
  0.0 0.9 %copy-start = (bf16[32,2048]{1,0:T(8,128)(2,1)S(1)}, bf16[32,2048]{1,0:T(8,128)(2,1)}, u32[]{:S(2)}) copy-start(bf16[32,2048]{1,0:T(8,128)(2,1)} %t_hbm.1) | copy-start | bytes 393220

commit v5 on v4

--- a/solution.py
+++ b/solution.py
@@ -100,6 +100,12 @@
         sent.append(c)
 
     def block(ph, h, mx, dz, piece, origin=False):
+        if piece == "w":
+            if ph == C:
+                return cb.at[h, cslot(h, mx, dz)]
+            if origin and not mx and dz == 0:
+                return t_hbm.at[pl.ds(16 * h, 16)]
+            return tslot(h, k, mx, dz)
         if ph == A:
             cut = pl.ds(0, CUT_A) if piece == "x" else pl.ds(CUT_A, 2048 - CUT_A)
             if origin and not mx and dz == 0:
@@ -116,8 +122,8 @@
         sign = 1 if way == 0 else -1
         if kind == "E":
             return (ph, h, False, -sign * 3, "z"), (ph, h, True, -sign * 4, "z"), i, 28, xzdev(sign)
-        mx, piece = kind == "p", "z" if kind == "z" else "x"
-        n = "zxp".index(kind) * 8 + way * 4 + d - 1
+        mx, piece = kind == "p", "w" if kind == "w" else "x"
+        n = "wxp".index(kind) * 8 + way * 4 + d - 1
         if kind == "p" and d == 1:
             return (ph, h, False, 0, piece), (ph, h, True, -sign, piece), i, n, xzdev(sign)
         return (ph, h, mx, -sign * (d - 1), piece), (ph, h, mx, -sign * d, piece), i, n, zdev(sign)
@@ -135,7 +141,7 @@
         return d <= 3 or (d == 4 and (way == h) == (kind != "p"))
 
     def ag_start(ph, h):
-        for kind in "pzx":
+        for kind in "pw":
             for way in (0, 1):
                 send(ph, h, kind, way, 1)
         send(ph, h, "Y", 0, 0)
@@ -147,13 +153,13 @@
                 arrived(ph, h, kind, way, d)
                 if exists(h, kind, way, d + 1):
                     send(ph, h, kind, way, d + 1)
-                if kind == "z" and d == 3 and way == h:
+                if kind == "w" and d == 3 and way == h:
                     send(ph, h, "E", way, 4)
-                if kind == "z" and d < 4:
+                if kind == "w" and d < 4:
                     send(ph, h, "X", 0, -d if way == 0 else d)
 
     def step(ph, h, d):
-        for kind in "zpx":
+        for kind in "wp":
             ag(ph, h, kind, d)
 
     def around(d):

time: 80.6 us -> 82.6 us (1.025)
  Pallas kernels: 78.9 us -> 81 us
    pallas_call x1, Pallas kernels: 78.9 us -> 81 us  [body(): pl.pallas_call(kernel, out_shape=jax.ShapeDtypeStruct((32, 512), f32), in...]
where the time goes in v5:
time: 82.6 us
  Pallas kernels  81 us (98%)
  local copies, waits for them, and re-layouts  1.54 us (2%)
    pallas_call x1, Pallas kernels, body(): pl.pallas_call(kernel, out_shape=jax.ShapeDtypeStruct((32, 512), f32), in...  81 us

profile of v5, /device:TPU:1, one launch (start us, length us, event | category | flops | bytes accessed | tf_op | source)
XLA Modules:
  0.0 82.6 jit_solution(14095915122188172840)
XLA Ops:
  0.0 0.0 copy-start
  0.0 0.9 %copy-done = bf16[32,2048]{1,0:T(8,128)(2,1)S(1)} copy-done((bf16[32,2048]{1,0:T(8,128)(2,1)S(1)}, bf16[32,2048]{1,0:T(8,128)(2,1)}, u32[]{:S(2)}) %copy-start) | copy-done | bytes 131096
  0.9 81.0 %scores_kernel.1 = f32[32,512]{1,0:T(8,128)S(1)} custom-call(bf16[32,2048]{1,0:T(8,128)(2,1)S(1)} %copy-done, bf16[2048,2048]{1,0:T(8,128)(2,1)} %g_hbm.1, bf16[512,2048]{1,0:T(8,128)(2,1)} %d_hbm.1), custom_call_target="tpu_custom_call" | custom-call | flops 5400000000 | bytes 11000000 | tf_op jit(solution)/shard_map/scores_kernel/pallas_call | solution.py:360
  81.9 0.6 copy.5
Async XLA Ops:
  0.0 0.9 %copy-start = (bf16[32,2048]{1,0:T(8,128)(2,1)S(1)}, bf16[32,2048]{1,0:T(8,128)(2,1)}, u32[]{:S(2)}) copy-start(bf16[32,2048]{1,0:T(8,128)(2,1)} %t_hbm.1) | copy-start | bytes 393220
